TPU v7x, 256 devices: a whole 4x4x8 slice. The times are simulated.
256 devices in a mesh: dp: 64 (over y, z, core), tensor: 4 (over x).
Axes of the slice: x: 4, y: 4, z: 8, core: 2. Of those that a mesh axis runs over, the one named last changes fastest.
Arguments:
- activations: bfloat16 [65536, 4096], P(('dp', 'tensor')), may hold values from -6 to 6
- cotangent: bfloat16 [2, 65536, 1024], P(None, 'dp', 'tensor'), may hold values from -0.19921875 to 0.19921875
- error_memory: bfloat16 [2, 64, 4096, 1024], P(None, 'dp', None, 'tensor'), may hold values from -3 to 3
- right_factor: float32 [2, 1024, 32], P(None, 'tensor'), may hold values from -6 to 6
Outputs:
- new_error: bfloat16 [2, 64, 4096, 1024], P(None, 'dp', None, 'tensor')
- left_factor: float32 [2, 4, 4096, 32], P(None, 'tensor')
- mean_right: float32 [2, 1024, 32], P(None, 'tensor')
All inputs are finite; a program needn't handle non-finite values.
Results may differ from a plain program's by a relative error of at most 0.00045.
Values may be sent and summed in bfloat16 or wider, within the bound.
A program may use at most 128 MiB of HBM per device.

v0:
```python
import functools

import jax
import jax.numpy as jnp
from jax import lax
from jax.experimental import pallas as pl
from jax.experimental.pallas import tpu as pltpu
from jax.sharding import PartitionSpec as P

MESH = pl.DeviceIdType.MESH
BF = jnp.bfloat16
F32 = jnp.float32
NX = 4
RANK = 32
NT = (((1,), (1,)), ((), ()))
TN = (((0,), (0,)), ((), ()))


def split(value):
    high = value.astype(BF)
    return high, (value - high.astype(F32)).astype(BF)


def dot(a, b, dims=None):
    if dims is None:
        dims = (((1,), (0,)), ((), ()))
    return lax.dot_general(a, b, dims, preferred_element_type=F32)


def inverse_factor(gram):
    rows = lax.broadcasted_iota(jnp.int32, (RANK, 2 * RANK), 0)
    cols = lax.broadcasted_iota(jnp.int32, (RANK, 2 * RANK), 1)
    eye = jnp.where(cols == rows + RANK, 1.0, 0.0).astype(F32)
    wide = jnp.concatenate([gram, jnp.zeros((RANK, RANK), F32)], axis=1) + eye
    index = rows[:, :1]
    pivots = jnp.ones((RANK, 1), F32)
    for j in range(RANK):
        row = wide[j:j + 1, :]
        pivot = wide[j:j + 1, j:j + 1]
        column = wide[:, j:j + 1]
        factor = jnp.where(index > j, column * (1.0 / pivot), 0.0)
        pivots = jnp.where(index == j, pivot, pivots)
        wide = wide - factor * row
    return wide[:, RANK:] * (1.0 / jnp.sqrt(pivots))


def fused(NY, NZ, a_hbm, c_hbm, e_hbm, rt_hbm, mem_hbm, left_hbm, mean_ref,
          a, c, e, rt, v, vall, vl, rb, p, rc, fy, ry, q, rz, sp, rx, s, sb, left, mem, t, ta, t2, ty, tf,
          lsem, vs, vr, xs, xr, cs, cr, fs, fr, ys, yr, zs, zr, ws, wr, gzs, gzr, gys, gyr, gcs, gcr,
          tas, tar, tys, tyr, tgs, tgr):
    dp, x = lax.axis_index("dp"), lax.axis_index("tensor")
    core, yz = lax.rem(dp, 2), lax.div(dp, 2)
    z, y = lax.rem(yz, NZ), lax.div(yz, NZ)
    other = 1 - core
    tokens = a.shape[1]
    width = a.shape[2]
    kv = c.shape[2]
    span = NY * 128
    ndp = 2 * NY * NZ

    def at_x(k):
        return {"dp": dp, "tensor": lax.rem(x + k, NX)}

    def at_y(k):
        return {"dp": (lax.rem(y + k, NY) * NZ + z) * 2 + core, "tensor": x}

    def at_zc(zz, cc):
        return {"dp": (y * NZ + zz) * 2 + cc, "tensor": x}

    def at_z(zz):
        return at_zc(zz, core)

    partner = at_zc(z, other)
    plane = [(d, k) for d in range(2) for k in range(NZ) if d + k]

    def remote(src, dst, send, recv, device):
        return pltpu.make_async_remote_copy(src_ref=src, dst_ref=dst, send_sem=send, recv_sem=recv,
                                            device_id=device, device_id_type=MESH)

    load_a = pltpu.make_async_copy(a_hbm, a.at[x], lsem.at[0])
    load_c = pltpu.make_async_copy(c_hbm, c, lsem.at[1])
    load_e = pltpu.make_async_copy(e_hbm, e, lsem.at[2])
    load_r = pltpu.make_async_copy(rt_hbm, rt, lsem.at[3])
    load_r.start()
    load_c.start()
    load_a.start()
    load_e.start()

    barrier = pltpu.get_barrier_semaphore()
    for k in range(1, NX):
        pl.semaphore_signal(barrier, inc=1, device_id=at_x(k), device_id_type=MESH)
    for k in range(1, NY):
        pl.semaphore_signal(barrier, inc=1, device_id=at_y(k), device_id_type=MESH)
    for d, k in plane:
        pl.semaphore_signal(barrier, inc=1, device_id=at_zc(lax.rem(z + k, NZ), (core, other)[d]), device_id_type=MESH)

    load_r.wait()
    load_c.wait()
    for m in range(2):
        high, low = split(rt[m])
        rb[m] = jnp.concatenate([high, low], axis=0)
        both = dot(rb[m], c[m], NT)
        vt = both[:RANK] + both[RANK:]
        for b in range(NX):
            v[b, m * RANK:(m + 1) * RANK, :] = vt[:, b * tokens:(b + 1) * tokens]

    pl.semaphore_wait(barrier, NX + NY + 2 * NZ - 3)

    v_copies = []
    for k in range(1, NX):
        copy = remote(v.at[lax.rem(x + k, NX)], vall.at[x], vs.at[k - 1], vr.at[k - 1], at_x(k))
        copy.start()
        v_copies.append(copy)

    quarter = tokens // 4
    left_x, right_x = lax.rem(x + NX - 1, NX), lax.rem(x + 1, NX)
    far_x = lax.rem(x + 2, NX)
    right_dev, left_dev = at_x(1), at_x(NX - 1)

    def quarter_copy(slot, i, sem, device):
        part = a.at[slot, pl.ds(i * quarter, quarter)]
        return remote(part, part, xs.at[sem], xr.at[sem], device)

    to_right = [quarter_copy(x, i, i, right_dev) for i in range(4)]
    to_left = [quarter_copy(x, i, 4 + i, left_dev) for i in (2, 3, 0, 1)]
    forward_right = [quarter_copy(left_x, i, 8 + i, right_dev) for i in range(2)]
    forward_left = [quarter_copy(right_x, 2 + i, 10 + i, left_dev) for i in range(2)]
    load_a.wait()
    for i in range(2):
        to_right[i].start()
        to_left[i].start()

    def left_arrived(parts):
        for i in parts:
            quarter_copy(left_x, i, i, right_dev).wait_recv()

    def right_arrived(parts):
        for i in parts:
            quarter_copy(right_x, i, 4 + i, right_dev).wait_recv()

    def far_arrived():
        for i in range(2):
            quarter_copy(far_x, i, 8 + i, right_dev).wait_recv()
            quarter_copy(far_x, 2 + i, 10 + i, right_dev).wait_recv()

    vall[x] = v[x]
    for k in range(1, NX):
        src = lax.rem(x + NX - k, NX)
        remote(v.at[0], vall.at[src], vs.at[k - 1], vr.at[k - 1], at_x(k)).wait_recv()
    stacked = jnp.concatenate(
        [vall[b, m * RANK:(m + 1) * RANK, :] for m in range(2) for b in range(NX)], axis=0)
    high, low = split(stacked)
    block = 2 * NX * RANK
    vl[:block] = high
    vl[block:] = low

    load_e.wait()

    def partials(j, carry):
        zj = lax.rem(z + 1 + j, NZ)
        at = pl.ds(pl.multiple_of(zj * span, span), span)
        both = dot(vl[...], a[x, :, at])
        both = both[:block] + both[block:]
        for m in range(2):
            for yb in range(NY):
                for b in range(NX):
                    r0 = (m * NX + b) * RANK
                    p[m, zj, yb, b] = both[r0:r0 + RANK, yb * 128:(yb + 1) * 128]
        for m in range(2):
            et = dot(rb[m], e[m, at, :], NT)
            et = et[:RANK] + et[RANK:]
            for yb in range(NY):
                p[m, zj, yb, x] = p[m, zj, yb, x] + et[:, yb * 128:(yb + 1) * 128]
        remote(p.at[other, zj], rc.at[zj], cs.at[zj], cr.at[zj], partner).start()
        return carry

    lax.fori_loop(0, NZ, partials, 0)

    hc = NX // 2
    up, down, far_y = lax.rem(y + 1, NY), lax.rem(y + NY - 1, NY), lax.rem(y + 2, NY)
    to_up, to_down = at_y(1), at_y(NY - 1)

    def over_cores(j, carry):
        zj = lax.rem(z + 1 + j, NZ)
        remote(p.at[other, zj], rc.at[zj], cs.at[zj], cr.at[zj], partner).wait_recv()
        p[core, zj] = p[core, zj] + rc[zj]
        remote(p.at[core, zj, far_y, pl.ds(0, hc)], fy.at[0, zj], fs.at[0, zj], fr.at[0, zj], to_up).start()
        remote(p.at[core, zj, far_y, pl.ds(hc, hc)], fy.at[1, zj], fs.at[1, zj], fr.at[1, zj], to_down).start()
        return carry

    lax.fori_loop(0, NZ, over_cores, 0)

    to_right[2].start()
    to_left[2].start()

    def to_neighbours(j, carry):
        zj = lax.rem(z + 1 + j, NZ)
        for i, target, device in ((0, up, to_up), (1, down, to_down)):
            part = pl.ds(i * hc, hc)
            remote(p.at[core, zj, far_y, part], fy.at[i, zj], fs.at[i, zj], fr.at[i, zj], device).wait_recv()
            p[core, zj, target, part] = p[core, zj, target, part] + fy[i, zj]
            remote(p.at[core, zj, target], ry.at[i, zj], ys.at[i, zj], yr.at[i, zj], device).start()
        return carry

    lax.fori_loop(0, NZ, to_neighbours, 0)

    step = min(512, width)

    def accumulate(slot, first):
        tok = pl.ds(pl.multiple_of(slot * tokens, tokens), tokens)
        cc = jnp.concatenate([c[0, tok, :], c[1, tok, :]], axis=1)

        def body(i, carry):
            at = pl.ds(pl.multiple_of(i * step, step), step)
            g = dot(a[slot, :, at], cc, TN)
            for m in range(2):
                base = e[m, at, :].astype(F32) if first else mem[m, at, :]
                mem[m, at, :] = base + g[:, m * kv:(m + 1) * kv]
            return carry

        lax.fori_loop(0, width // step, body, 0)

    accumulate(x, True)

    def over_y(zj):
        total = p[core, zj, y]
        for i in range(2):
            remote(p.at[core, zj, y], ry.at[i, zj], ys.at[i, zj], yr.at[i, zj], partner).wait_recv()
            total = total + ry[i, zj]
        q[zj] = total

    def over_y_send(j, carry):
        zj = lax.rem(z + 1 + j, NZ)
        over_y(zj)
        remote(q.at[zj], rz.at[j], zs.at[j], zr.at[j], at_z(zj)).start()
        return carry

    lax.fori_loop(0, NZ - 1, over_y_send, 0)
    over_y(z)

    total = q[z]
    for j in range(NZ - 1):
        remote(q.at[z], rz.at[j], zs.at[j], zr.at[j], partner).wait_recv()
        total = total + rz[j]
    sp[...] = total

    for k in range(1, NX):
        remote(sp.at[lax.rem(x + k, NX)], rx.at[k - 1], ws.at[k - 1], wr.at[k - 1], at_x(k)).start()
    to_right[3].start()
    to_left[3].start()
    for i in range(2):
        left_arrived([i])
        forward_right[i].start()
        right_arrived([2 + i])
        forward_left[i].start()
    total = sp[x]
    for k in range(1, NX):
        remote(sp.at[0], rx.at[k - 1], ws.at[k - 1], wr.at[k - 1], at_x(k)).wait_recv()
        total = total + rx[k - 1]
    s[core, z, y] = total

    own = s.at[core, z, y]
    for k in range(1, NZ):
        remote(own, own, gzs.at[k - 1], gzr.at[k - 1], at_z(lax.rem(z + k, NZ))).start()
    for k in range(1, NZ):
        got = s.at[core, lax.rem(z + NZ - k, NZ), y]
        remote(got, got, gzs.at[k - 1], gzr.at[k - 1], partner).wait_recv()
    own_y = s.at[core, :, y]
    hz = NZ // 2
    remote(own_y, own_y, gys.at[0], gyr.at[0], to_up).start()
    remote(own_y, own_y, gys.at[1], gyr.at[1], to_down).start()
    pass_up, pass_down = s.at[core, pl.ds(0, hz), down], s.at[core, pl.ds(hz, hz), up]
    remote(s.at[core, :, down], s.at[core, :, down], gys.at[0], gyr.at[0], to_up).wait_recv()
    remote(pass_up, pass_up, gys.at[2], gyr.at[2], to_up).start()
    remote(s.at[core, :, up], s.at[core, :, up], gys.at[1], gyr.at[1], to_down).wait_recv()
    remote(pass_down, pass_down, gys.at[3], gyr.at[3], to_down).start()
    for i in range(2):
        got = s.at[core, pl.ds(i * hz, hz), far_y]
        remote(got, got, gys.at[2 + i], gyr.at[2 + i], partner).wait_recv()
    remote(s.at[core], s.at[core], gcs.at[0], gcr.at[0], partner).start()
    remote(s.at[other], s.at[other], gcs.at[0], gcr.at[0], partner).wait_recv()

    for m in range(2):
        for zz in range(NZ):
            for yy in range(NY):
                d0 = (zz * NY + yy) * 128
                high, low = split(s[m, zz, yy])
                sb[m * 64:m * 64 + 32, d0:d0 + 128] = high
                sb[m * 64 + 32:m * 64 + 64, d0:d0 + 128] = low

    right = []
    for m in range(2):
        both = dot(sb[m * 64:m * 64 + 64, :], e[m])
        right.append(both[:RANK] + both[RANK:])

    def project(slot):
        tok = pl.ds(pl.multiple_of(slot * tokens, tokens), tokens)
        u = dot(sb[...], a[slot], NT)
        for m in range(2):
            high, low = split(u[m * 64:m * 64 + 32] + u[m * 64 + 32:m * 64 + 64])
            both = dot(jnp.concatenate([high, low], axis=0), c[m, tok, :])
            right[m] = right[m] + both[:RANK] + both[RANK:]

    project(x)

    inverse = []
    for m in range(2):
        both = dot(sb[m * 64:m * 64 + 64, :], sb[m * 64:m * 64 + 64, :], NT)
        inverse.append(inverse_factor(
            both[:RANK, :RANK] + both[:RANK, RANK:] + both[RANK:, :RANK] + both[RANK:, RANK:]))
    for m in range(2):
        high, low = split(inverse[m])
        pair = jnp.concatenate([high, low], axis=0)
        for i in range(width // step):
            at = pl.ds(i * step, step)
            both = dot(pair, sb[m * 64:m * 64 + 32, at])
            left[m, :, at] = both[:RANK] + both[RANK:] + dot(high, sb[m * 64 + 32:m * 64 + 64, at])
    store_left = pltpu.make_async_copy(left, left_hbm, lsem.at[4])
    store_left.start()

    left_arrived([2, 3])
    project(left_x)
    accumulate(left_x, False)
    right_arrived([0, 1])
    project(right_x)
    accumulate(right_x, False)
    far_arrived()
    project(far_x)

    group = t.shape[2]
    per_row = kv // 128

    def piece(i):
        return i // group, i % group

    for m in range(2):
        for i in range(NZ * group):
            rr, kk = i // per_row, i % per_row
            t[(m,) + piece(i)] = right[m][rr * 8:rr * 8 + 8, kk * 128:kk * 128 + 128]
    for i, (d, k) in enumerate(plane):
        zk, ck = lax.rem(z + k, NZ), (core, other)[d]
        remote(t.at[ck, zk], ta.at[i], tas.at[i], tar.at[i], at_zc(zk, ck)).start()
    accumulate(far_x, False)
    store_mem = pltpu.make_async_copy(mem, mem_hbm, lsem.at[5])
    store_mem.start()
    total = t[core, z]
    for i in range(len(plane)):
        remote(t.at[core, z], ta.at[i], tas.at[i], tar.at[i], partner).wait_recv()
        total = total + ta[i]
    t2[...] = total
    for k in range(1, NY):
        remote(t2, ty.at[k - 1], tys.at[k - 1], tyr.at[k - 1], at_y(k)).start()
    for k in range(1, NY):
        remote(t2, ty.at[k - 1], tys.at[k - 1], tyr.at[k - 1], partner).wait_recv()
        total = total + ty[k - 1]
    tf[core, z] = total
    own_t = tf.at[core, z]
    for i, (d, k) in enumerate(plane):
        remote(own_t, own_t, tgs.at[i], tgr.at[i], at_zc(lax.rem(z + k, NZ), (core, other)[d])).start()
    for i, (d, k) in enumerate(plane):
        got = tf.at[(core, other)[d], lax.rem(z + NZ - k, NZ)]
        remote(got, got, tgs.at[i], tgr.at[i], partner).wait_recv()

    for m in range(2):
        tt = jnp.concatenate(
            [jnp.concatenate([tf[(m,) + piece(rr * per_row + kk)] for kk in range(per_row)], axis=1)
             for rr in range(RANK // 8)], axis=0)
        wh, wl = split(inverse[m])
        th, tl = split(tt)
        both = dot(jnp.concatenate([wh, wl], axis=0), th)
        mean_ref[m] = (both[:RANK] + both[RANK:] + dot(wh, tl)) * (1.0 / ndp)

    for copy in v_copies + to_right + to_left + forward_right + forward_left:
        copy.wait_send()

    def sent(j, carry):
        remote(p.at[other, j], rc.at[j], cs.at[j], cr.at[j], partner).wait_send()
        for i in range(2):
            remote(fy.at[i, j], fy.at[i, j], fs.at[i, j], fr.at[i, j], partner).wait_send()
            remote(p.at[core, j, y], ry.at[i, j], ys.at[i, j], yr.at[i, j], partner).wait_send()
        return carry

    lax.fori_loop(0, NZ, sent, 0)
    own = s.at[core, z, y]
    for j in range(NZ - 1):
        remote(q.at[j], rz.at[j], zs.at[j], zr.at[j], partner).wait_send()
        remote(own, own, gzs.at[j], gzr.at[j], partner).wait_send()
    for k in range(NX - 1):
        remote(sp.at[0], rx.at[k], ws.at[k], wr.at[k], partner).wait_send()
    for i in range(2):
        remote(own_y, own_y, gys.at[i], gyr.at[i], partner).wait_send()
    remote(pass_up, pass_up, gys.at[2], gyr.at[2], partner).wait_send()
    remote(pass_down, pass_down, gys.at[3], gyr.at[3], partner).wait_send()
    remote(s.at[core], s.at[core], gcs.at[0], gcr.at[0], partner).wait_send()
    for i in range(len(plane)):
        remote(t2, ta.at[i], tas.at[i], tar.at[i], partner).wait_send()
        remote(own_t, own_t, tgs.at[i], tgr.at[i], partner).wait_send()
    for k in range(NY - 1):
        remote(t2, ty.at[k], tys.at[k], tyr.at[k], partner).wait_send()
    store_left.wait()
    store_mem.wait()


def residual(parts, mem_hbm, left_hbm, mean_ref, out_hbm, left_out, mean_out,
             mem, left, out, load_sem, store_sem, left_sem):
    rows = mem.shape[1] // parts
    blocks = [(m, pl.ds(i * rows, rows), m * parts + i) for m in range(2) for i in range(parts)]
    load_left = pltpu.make_async_copy(left_hbm, left, left_sem.at[0])
    load_left.start()
    loads = [pltpu.make_async_copy(mem_hbm.at[m, at], mem.at[m, at], load_sem.at[i]) for m, at, i in blocks]
    stores = [pltpu.make_async_copy(out.at[m, at], out_hbm.at[m, at], store_sem.at[i]) for m, at, i in blocks]
    for load in loads:
        load.start()
    store_left = pltpu.make_async_copy(left, left_out, left_sem.at[1])
    load_left.wait()
    store_left.start()
    mean_out[...] = mean_ref[...]
    for m, at, i in blocks:
        lh, ll = split(left[m, :, at])
        mh, ml = split(mean_ref[m])
        approx = dot(jnp.concatenate([lh, ll, lh], axis=0), jnp.concatenate([mh, mh, ml], axis=0), TN)
        loads[i].wait()
        out[m, at, :] = (mem[m, at, :] - approx).astype(BF)
        stores[i].start()
    for store in stores:
        store.wait()
    store_left.wait()


def shards(NY, NZ, activations, cotangent, error_memory, right_factor):
    tokens, width = activations.shape
    kv = cotangent.shape[2]
    error_memory = error_memory[:, 0]
    group = RANK * kv // (8 * 128 * NZ)
    dma = pltpu.SemaphoreType.DMA
    any_spec = pl.BlockSpec(memory_space=pl.ANY)
    mem, left, mean = pl.pallas_call(
        functools.partial(fused, NY, NZ),
        out_shape=(
            jax.ShapeDtypeStruct((2, width, kv), F32),
            jax.ShapeDtypeStruct((2, RANK, width), F32),
            jax.ShapeDtypeStruct((2, RANK, kv), F32),
        ),
        in_specs=[any_spec] * 4,
        out_specs=(any_spec, any_spec, pl.BlockSpec(memory_space=pltpu.VMEM)),
        scratch_shapes=[
            pltpu.VMEM((NX, tokens, width), BF),
            pltpu.VMEM((2, NX * tokens, kv), BF),
            pltpu.VMEM((2, width, kv), BF),
            pltpu.VMEM((2, RANK, kv), F32),
            pltpu.VMEM((NX, 2 * RANK, tokens), F32),
            pltpu.VMEM((NX, 2 * RANK, tokens), F32),
            pltpu.VMEM((4 * NX * RANK, tokens), BF),
            pltpu.VMEM((2, 2 * RANK, kv), BF),
            pltpu.VMEM((2, NZ, NY, NX, RANK, 128), F32),
            pltpu.VMEM((NZ, NY, NX, RANK, 128), F32),
            pltpu.VMEM((2, NZ, NX // 2, RANK, 128), F32),
            pltpu.VMEM((2, NZ, NX, RANK, 128), F32),
            pltpu.VMEM((NZ, NX, RANK, 128), F32),
            pltpu.VMEM((NZ - 1, NX, RANK, 128), F32),
            pltpu.VMEM((NX, RANK, 128), F32),
            pltpu.VMEM((NX - 1, RANK, 128), F32),
            pltpu.VMEM((2, NZ, NY, RANK, 128), F32),
            pltpu.VMEM((4 * RANK, width), BF),
            pltpu.VMEM((2, RANK, width), F32),
            pltpu.VMEM((2, width, kv), F32),
            pltpu.VMEM((2, NZ, group, 8, 128), F32),
            pltpu.VMEM((2 * NZ - 1, group, 8, 128), F32),
            pltpu.VMEM((group, 8, 128), F32),
            pltpu.VMEM((NY - 1, group, 8, 128), F32),
            pltpu.VMEM((2, NZ, group, 8, 128), F32),
            dma((6,)),
            dma((NX - 1,)), dma((NX - 1,)),
            dma((12,)), dma((12,)),
            dma((NZ,)), dma((NZ,)),
            dma((2, NZ)), dma((2, NZ)),
            dma((2, NZ)), dma((2, NZ)),
            dma((NZ - 1,)), dma((NZ - 1,)),
            dma((NX - 1,)), dma((NX - 1,)),
            dma((NZ - 1,)), dma((NZ - 1,)),
            dma((4,)), dma((4,)),
            dma((1,)), dma((1,)),
            dma((2 * NZ - 1,)), dma((2 * NZ - 1,)),
            dma((NY - 1,)), dma((NY - 1,)),
            dma((2 * NZ - 1,)), dma((2 * NZ - 1,)),
        ],
        compiler_params=pltpu.CompilerParams(
            collective_id=0, has_side_effects=True, vmem_limit_bytes=56 * 1024 * 1024),
    )(activations, cotangent, error_memory, jnp.swapaxes(right_factor, 1, 2))

    parts = 4
    vmem_spec = pl.BlockSpec(memory_space=pltpu.VMEM)
    new_error, left, mean = pl.pallas_call(
        functools.partial(residual, parts),
        out_shape=(
            jax.ShapeDtypeStruct((2, width, kv), BF),
            jax.ShapeDtypeStruct((2, RANK, width), F32),
            jax.ShapeDtypeStruct((2, RANK, kv), F32),
        ),
        in_specs=[any_spec, any_spec, vmem_spec],
        out_specs=(any_spec, any_spec, vmem_spec),
        scratch_shapes=[
            pltpu.VMEM((2, width, kv), F32),
            pltpu.VMEM((2, RANK, width), F32),
            pltpu.VMEM((2, width, kv), BF),
            dma((2 * parts,)),
            dma((2 * parts,)),
            dma((2,)),
        ],
        compiler_params=pltpu.CompilerParams(vmem_limit_bytes=56 * 1024 * 1024),
    )(mem, left, mean)
    return (new_error[:, None], jnp.swapaxes(left, 1, 2)[:, None], jnp.swapaxes(mean, 1, 2))


def build(mesh, NY, NZ):
    return jax.shard_map(
        functools.partial(shards, NY, NZ),
        mesh=mesh,
        in_specs=(
            P(("dp", "tensor"), None),
            P(None, "dp", "tensor"),
            P(None, "dp", None, "tensor"),
            P(None, "tensor", None),
        ),
        out_specs=(
            P(None, "dp", None, "tensor"),
            P(None, "tensor", None, None),
            P(None, "tensor", None),
        ),
        check_vma=False,
    )


def solution(mesh):
    return build(mesh, 4, mesh.shape["dp"] // 8)
```

profile of v0, /device:TPU:1, one launch (start us, length us, event | category | flops | bytes accessed | tf_op | source)
XLA Modules:
  0.0 112.2 jit_solution(2726105671255228729)
XLA Ops:
  0.6 101.7 %shard_map.67 = (f32[2,4096,256]{2,1,0:T(8,128)}, f32[2,32,4096]{2,1,0:T(8,128)}, f32[2,32,256]{2,1,0:T(8,128)}) custom-call(bf16[256,4096]{1,0:T(8,128)(2,1)} %a_hbm.1, bf16[2,1024,256]{2,1,0:T(8,128)(2,1)} %c_hbm.1, bf16[2,4096,256]{2,1,0:T(8,128)(2,1)} %bitcast.11, f32[2,32,256]{2,1,0:T(8,128)} %bitcast.12), custom_call_target="tpu_custom_call" | custom-call | tf_op jit(solution)/shard_map/pallas_call | solution.py:437
  102.4 9.8 %shard_map.68 = (bf16[2,4096,256]{2,1,0:T(8,128)(2,1)}, f32[2,32,4096]{2,1,0:T(8,128)}, f32[2,32,256]{2,1,0:T(8,128)}) custom-call(f32[2,4096,256]{2,1,0:T(8,128)} %get-tuple-element.9.mem_hbm, f32[2,32,4096]{2,1,0:T(8,128)} %get-tuple-element.10.left_hbm, f32[2,32,256]{2,1,0:T(8,128)} %get-tuple-element.11.mean_ref), custom_call_target="tpu_custom_call" | custom-call | tf_op jit(solution)/shard_map/pallas_call | solution.py:493
where the time goes:
time: 112 us
  Pallas kernels  112 us (100%)
    pallas_call x1, Pallas kernels, shards(): pl.pallas_call(functools.partial(fused, NY, NZ), out_shape=(jax.ShapeDtyp...  102 us
    pallas_call x1, Pallas kernels, shards(): pl.pallas_call(functools.partial(residual, parts), out_shape=(jax.ShapeDt...  9.81 us

commit v1 on v0

--- a/solution.py
+++ b/solution.py
@@ -45,7 +45,7 @@
 
 
 def fused(NY, NZ, a_hbm, c_hbm, e_hbm, rt_hbm, mem_hbm, left_hbm, mean_ref,
-          a, c, e, rt, v, vall, vl, rb, p, rc, fy, ry, q, rz, sp, rx, s, sb, left, mem, t, ta, t2, ty, tf,
+          a, c, e, rt, v, vall, vl, rb, pe, p, rc, fy, ry, q, rz, sp, rx, s, sb, left, mem, t, ta, t2, ty, tf,
           lsem, vs, vr, xs, xr, cs, cr, fs, fr, ys, yr, zs, zr, ws, wr, gzs, gzr, gys, gyr, gcs, gcr,
           tas, tar, tys, tyr, tgs, tgr):
     dp, x = lax.axis_index("dp"), lax.axis_index("tensor")
@@ -143,6 +143,19 @@
             quarter_copy(far_x, i, 8 + i, right_dev).wait_recv()
             quarter_copy(far_x, 2 + i, 10 + i, right_dev).wait_recv()
 
+    load_e.wait()
+
+    def error_part(j, carry):
+        at = pl.ds(pl.multiple_of(j * span, span), span)
+        for m in range(2):
+            et = dot(rb[m], e[m, at, :], NT)
+            et = et[:RANK] + et[RANK:]
+            for yb in range(NY):
+                pe[m, j, yb] = et[:, yb * 128:(yb + 1) * 128]
+        return carry
+
+    lax.fori_loop(0, NZ, error_part, 0)
+
     vall[x] = v[x]
     for k in range(1, NX):
         src = lax.rem(x + NX - k, NX)
@@ -154,9 +167,7 @@
     vl[:block] = high
     vl[block:] = low
 
-    load_e.wait()
-
-    def partials(j, carry):
+    def partials(j):
         zj = lax.rem(z + 1 + j, NZ)
         at = pl.ds(pl.multiple_of(zj * span, span), span)
         both = dot(vl[...], a[x, :, at])
@@ -167,28 +178,29 @@
                     r0 = (m * NX + b) * RANK
                     p[m, zj, yb, b] = both[r0:r0 + RANK, yb * 128:(yb + 1) * 128]
         for m in range(2):
-            et = dot(rb[m], e[m, at, :], NT)
-            et = et[:RANK] + et[RANK:]
             for yb in range(NY):
-                p[m, zj, yb, x] = p[m, zj, yb, x] + et[:, yb * 128:(yb + 1) * 128]
+                p[m, zj, yb, x] = p[m, zj, yb, x] + pe[m, zj, yb]
         remote(p.at[other, zj], rc.at[zj], cs.at[zj], cr.at[zj], partner).start()
-        return carry
-
-    lax.fori_loop(0, NZ, partials, 0)
 
     hc = NX // 2
     up, down, far_y = lax.rem(y + 1, NY), lax.rem(y + NY - 1, NY), lax.rem(y + 2, NY)
     to_up, to_down = at_y(1), at_y(NY - 1)
 
-    def over_cores(j, carry):
+    def over_cores(j):
         zj = lax.rem(z + 1 + j, NZ)
         remote(p.at[other, zj], rc.at[zj], cs.at[zj], cr.at[zj], partner).wait_recv()
         p[core, zj] = p[core, zj] + rc[zj]
         remote(p.at[core, zj, far_y, pl.ds(0, hc)], fy.at[0, zj], fs.at[0, zj], fr.at[0, zj], to_up).start()
         remote(p.at[core, zj, far_y, pl.ds(hc, hc)], fy.at[1, zj], fs.at[1, zj], fr.at[1, zj], to_down).start()
+
+    def staggered(j, carry):
+        partials(j)
+        over_cores(j - 1)
         return carry
 
-    lax.fori_loop(0, NZ, over_cores, 0)
+    partials(0)
+    lax.fori_loop(1, NZ, staggered, 0)
+    over_cores(NZ - 1)
 
     to_right[2].start()
     to_left[2].start()
@@ -402,29 +414,36 @@
 
 
 def residual(parts, mem_hbm, left_hbm, mean_ref, out_hbm, left_out, mean_out,
-             mem, left, out, load_sem, store_sem, left_sem):
+             mem, left, out, load_sem, store_sem, left_sem, left_out_sem):
     rows = mem.shape[1] // parts
     blocks = [(m, pl.ds(i * rows, rows), m * parts + i) for m in range(2) for i in range(parts)]
-    load_left = pltpu.make_async_copy(left_hbm, left, left_sem.at[0])
-    load_left.start()
-    loads = [pltpu.make_async_copy(mem_hbm.at[m, at], mem.at[m, at], load_sem.at[i]) for m, at, i in blocks]
+    flight = 3
+    loads = [(pltpu.make_async_copy(left_hbm.at[m, :, at], left.at[m, :, at], left_sem.at[i]),
+              pltpu.make_async_copy(mem_hbm.at[m, at], mem.at[m, at], load_sem.at[i])) for m, at, i in blocks]
     stores = [pltpu.make_async_copy(out.at[m, at], out_hbm.at[m, at], store_sem.at[i]) for m, at, i in blocks]
-    for load in loads:
-        load.start()
-    store_left = pltpu.make_async_copy(left, left_out, left_sem.at[1])
-    load_left.wait()
-    store_left.start()
+    stores_left = [pltpu.make_async_copy(left.at[m, :, at], left_out.at[m, :, at], left_out_sem.at[i])
+                   for m, at, i in blocks]
+    for i in range(flight):
+        for load in loads[i]:
+            load.start()
     mean_out[...] = mean_ref[...]
+    pairs = []
+    for m in range(2):
+        mh, ml = split(mean_ref[m])
+        pairs.append(jnp.concatenate([mh, mh, ml], axis=0))
     for m, at, i in blocks:
+        for load in loads[i]:
+            load.wait()
+        if i + flight < len(blocks):
+            for load in loads[i + flight]:
+                load.start()
         lh, ll = split(left[m, :, at])
-        mh, ml = split(mean_ref[m])
-        approx = dot(jnp.concatenate([lh, ll, lh], axis=0), jnp.concatenate([mh, mh, ml], axis=0), TN)
-        loads[i].wait()
+        approx = dot(jnp.concatenate([lh, ll, lh], axis=0), pairs[m], TN)
         out[m, at, :] = (mem[m, at, :] - approx).astype(BF)
         stores[i].start()
-    for store in stores:
+        stores_left[i].start()
+    for store in stores + stores_left:
         store.wait()
-    store_left.wait()
 
 
 def shards(NY, NZ, activations, cotangent, error_memory, right_factor):
@@ -452,6 +471,7 @@
             pltpu.VMEM((NX, 2 * RANK, tokens), F32),
             pltpu.VMEM((4 * NX * RANK, tokens), BF),
             pltpu.VMEM((2, 2 * RANK, kv), BF),
+            pltpu.VMEM((2, NZ, NY, RANK, 128), F32),
             pltpu.VMEM((2, NZ, NY, NX, RANK, 128), F32),
             pltpu.VMEM((NZ, NY, NX, RANK, 128), F32),
             pltpu.VMEM((2, NZ, NX // 2, RANK, 128), F32),
@@ -505,7 +525,8 @@
             pltpu.VMEM((2, width, kv), BF),
             dma((2 * parts,)),
             dma((2 * parts,)),
-            dma((2,)),
+            dma((2 * parts,)),
+            dma((2 * parts,)),
         ],
         compiler_params=pltpu.CompilerParams(vmem_limit_bytes=56 * 1024 * 1024),
     )(mem, left, mean)

time: 112 us -> 111 us (level)
  Pallas kernels: 112 us -> 110 us
    pallas_call x1, Pallas kernels: 9.81 us -> 8.24 us  [shards(): pl.pallas_call(functools.partial(residual, parts), out_shape=(jax.ShapeDt...]
where the time goes in v1:
time: 111 us
  Pallas kernels  110 us (99%)
    pallas_call x1, Pallas kernels, shards(): pl.pallas_call(functools.partial(fused, NY, NZ), out_shape=(jax.ShapeDtyp...  102 us
    pallas_call x1, Pallas kernels, shards(): pl.pallas_call(functools.partial(residual, parts), out_shape=(jax.ShapeDt...  8.24 us

profile of v1, /device:TPU:1, one launch (start us, length us, event | category | flops | bytes accessed | tf_op | source)
XLA Modules:
  0.0 110.6 jit_solution(16213179717450215876)
XLA Ops:
  0.6 101.7 %shard_map.67 = (f32[2,4096,256]{2,1,0:T(8,128)}, f32[2,32,4096]{2,1,0:T(8,128)}, f32[2,32,256]{2,1,0:T(8,128)}) custom-call(bf16[256,4096]{1,0:T(8,128)(2,1)} %a_hbm.1, bf16[2,1024,256]{2,1,0:T(8,128)(2,1)} %c_hbm.1, bf16[2,4096,256]{2,1,0:T(8,128)(2,1)} %bitcast.11, f32[2,32,256]{2,1,0:T(8,128)} %bitcast.12), custom_call_target="tpu_custom_call" | custom-call | tf_op jit(solution)/shard_map/pallas_call | solution.py:456
  102.4 8.2 %shard_map.68 = (bf16[2,4096,256]{2,1,0:T(8,128)(2,1)}, f32[2,32,4096]{2,1,0:T(8,128)}, f32[2,32,256]{2,1,0:T(8,128)}) custom-call(f32[2,4096,256]{2,1,0:T(8,128)} %get-tuple-element.9.mem_hbm, f32[2,32,4096]{2,1,0:T(8,128)} %get-tuple-element.10.left_hbm, f32[2,32,256]{2,1,0:T(8,128)} %get-tuple-element.11.mean_ref), custom_call_target="tpu_custom_call" | custom-call | tf_op jit(solution)/shard_map/pallas_call | solution.py:513
